TPU v7x, 32 devices: a whole 2x2x4 slice. The times are simulated.
32 devices in a mesh: groups: 2 (over y), lat: 4 (over z), row: 2 (over x), sub: 2 (over core).
Axes of the slice: x: 2, y: 2, z: 4, core: 2. Of those that a mesh axis runs over, the one named last changes fastest.
Arguments:
- target: bfloat16 [2048, 1536], P(('groups', 'lat', 'sub'), 'row'), parts along dimension 0, may hold values from -6 to 6
- dec_w: bfloat16 [16384, 1536], P(('groups', 'lat', 'sub'), 'row'), parts along dimension 0, may hold values from -0.4375 to 0.4375
- mom_first: bfloat16 [16384, 1536], P(('groups', 'lat', 'sub'), 'row'), parts along dimension 0, may hold values from -3 to 3
- mom_second: bfloat16 [16384, 1536], P(('groups', 'lat', 'sub'), 'row'), parts along dimension 0, may hold values from 0.0049743652 to 0.049804688
- ent_row: int32 [16, 2048], P(('groups', 'lat', 'sub')), parts along dimension 0, may hold values from 0 to 1023
- ent_lat: int32 [16, 2048], P(('groups', 'lat', 'sub')), parts along dimension 0, may hold values from 0 to 1023
- ent_val: bfloat16 [16, 2048], P(('groups', 'lat', 'sub')), parts along dimension 0, may hold values from 0 to 6, as said below
- block_count: int32 [16], P(('groups', 'lat', 'sub')), parts along dimension 0, may hold values from 1 to 16, as said below
Outputs:
- new_w: bfloat16 [16384, 1536], P(('groups', 'lat', 'sub'), 'row'), parts along dimension 0
- new_first: bfloat16 [16384, 1536], P(('groups', 'lat', 'sub'), 'row'), parts along dimension 0
- new_second: bfloat16 [16384, 1536], P(('groups', 'lat', 'sub'), 'row'), parts along dimension 0
There are 2 independent parts, one for each index of `groups`. A program takes and returns all parts, laid end to end along the dimension named above; each array names one. Nothing has to cross between parts.
Inputs may be any that keep to these rules, and one draw needn't show every extreme that they name: `block_count`: at least one latent shard uses all 16 blocks. `ent_val`: slots j >= 128 * block_count[q] of shard q hold zero.
All inputs are finite; a program needn't handle non-finite values.
Results may differ from a plain program's by a relative error of at most 0.0057.
Values may be sent and summed in bfloat16 or wider, within the bound.
A program may use at most 64 MiB of HBM per device.

v0:
```python
import functools
import jax
import jax.numpy as jnp
from jax import lax
from jax.experimental import pallas as pl
from jax.experimental.pallas import tpu as pltpu
from jax.sharding import PartitionSpec as P

BLOCK = 128
MESH = pl.DeviceIdType.MESH

beta_one = 0.9
beta_two = 0.999
learn_rate = 0.01
epsilon = 1e-08
correct_one = 0.999973438601112
correct_two = 0.095207852886291

CHUNK = 256
SPLIT = 2
LAG_MID = 3
LAG_ERR = 2
LAG_OUTER = 6


def adam_apply(weights, first_in, second_in, gradient):
    moment_one = beta_one * first_in.astype(jnp.float32) + (1.0 - beta_one) * gradient
    moment_two = beta_two * second_in.astype(jnp.float32) + (1.0 - beta_two) * gradient * gradient
    update = (
        learn_rate * (moment_one / correct_one) / (jnp.sqrt(moment_two / correct_two) + epsilon)
    )
    new_weights = (weights.astype(jnp.float32) - update).astype(jnp.bfloat16)
    return (new_weights, moment_one.astype(jnp.bfloat16), moment_two.astype(jnp.bfloat16))


def gradient_kernel(
    n, count_ref, row_ref, lat_ref, val_ref, w_ref, target_ref, g_ref,
    spread, pick, codes, part, own, err, sib_out, sib_in, in_out, up_in, mid_in,
    sib_s, sib_r, in_s, up_r, mid_r, out_s, out_r, err_s, err_r,
):
    z, c = lax.axis_index("lat"), lax.axis_index("sub")
    units, half, _ = own.shape
    unit = 2 * half
    share = target_ref.shape[0]
    slots = row_ref.shape[1]
    latents = w_ref.shape[0]
    side = z // (n // 2)
    inner, outer = z + 1 - 2 * side, z - 1 + 2 * side
    depth = z * (1 - side) + (n - 1 - z) * side
    is_end, is_mid = depth == 0, depth == n // 2 - 1
    not_end, not_mid = depth > 0, depth < n // 2 - 1
    sib_id, inner_id, outer_id = {"sub": 1 - c}, {"lat": inner}, {"lat": outer}

    barrier = pltpu.get_barrier_semaphore()
    pl.semaphore_signal(barrier, inc=1, device_id=sib_id, device_id_type=MESH)
    pl.semaphore_signal(barrier, inc=1, device_id=inner_id, device_id_type=MESH)

    @pl.when(not_end)
    def _():
        pl.semaphore_signal(barrier, inc=1, device_id=outer_id, device_id_type=MESH)
        pl.semaphore_wait(barrier, 3)

    @pl.when(is_end)
    def _():
        pl.semaphore_wait(barrier, 2)

    def rows_of(u, which):
        return pl.ds(pl.multiple_of(u * unit + which * half, 16), half)

    def sib_copy(u):
        return pltpu.make_async_remote_copy(
            src_ref=sib_out.at[u], dst_ref=sib_in.at[u], send_sem=sib_s.at[u],
            recv_sem=sib_r.at[u], device_id=sib_id, device_id_type=MESH)

    def up_copy(u):
        return pltpu.make_async_remote_copy(
            src_ref=in_out.at[u], dst_ref=up_in.at[u], send_sem=in_s.at[u],
            recv_sem=up_r.at[u], device_id=inner_id, device_id_type=MESH)

    def mid_copy(u):
        return pltpu.make_async_remote_copy(
            src_ref=in_out.at[u], dst_ref=mid_in.at[u], send_sem=in_s.at[u],
            recv_sem=mid_r.at[u], device_id=inner_id, device_id_type=MESH)

    def out_copy(u):
        return pltpu.make_async_remote_copy(
            src_ref=err.at[rows_of(u, c)], dst_ref=err.at[rows_of(u, c)], send_sem=out_s.at[u],
            recv_sem=out_r.at[u], device_id=outer_id, device_id_type=MESH)

    def err_copy(u, which):
        return pltpu.make_async_remote_copy(
            src_ref=err.at[rows_of(u, which)], dst_ref=err.at[rows_of(u, which)],
            send_sem=err_s.at[u], recv_sem=err_r.at[u], device_id=sib_id, device_id_type=MESH)

    live = lax.broadcasted_iota(jnp.int32, (1, slots), 1) < count_ref[0] * BLOCK
    values = jnp.where(live, val_ref[...].astype(jnp.float32), 0.0)

    @pl.loop(0, latents // BLOCK)
    def _(k):
        at = lax.broadcasted_iota(jnp.int32, (BLOCK, slots), 0) + k * BLOCK
        spread[pl.ds(pl.multiple_of(k * BLOCK, BLOCK), BLOCK), :] = jnp.where(
            at == lat_ref[...], values, 0.0
        ).astype(jnp.bfloat16)

    g_ref[...] = jnp.zeros_like(g_ref)

    def compute(b):
        rows = pl.ds(pl.multiple_of(b * CHUNK, CHUNK), CHUNK)
        at = lax.broadcasted_iota(jnp.int32, (CHUNK, slots), 0) + b * CHUNK
        pick[...] = jnp.where(at == row_ref[...], 1.0, 0.0).astype(jnp.bfloat16)
        codes[rows, :] = lax.dot_general(
            pick[...], spread[...], (((1,), (1,)), ((), ())), preferred_element_type=jnp.float32
        ).astype(jnp.bfloat16)
        part[...] = jnp.dot(codes[rows, :], w_ref[...], preferred_element_type=jnp.float32)
        first = (z * 2 + c) * share

        @pl.when(first // CHUNK == b)
        def _():
            at_own = pl.ds(pl.multiple_of(lax.rem(first, CHUNK), 16), share)
            part[at_own, :] = part[at_own, :] - target_ref[...].astype(jnp.float32)

        for j in range(SPLIT):
            u = b * SPLIT + j
            theirs = pl.ds(pl.multiple_of(j * unit + (1 - c) * half, 16), half)
            mine = pl.ds(pl.multiple_of(j * unit + c * half, 16), half)
            sib_out[u] = part[theirs, :].astype(jnp.bfloat16)
            sib_copy(u).start()
            own[u] = part[mine, :]

    def relay(u):
        sib_copy(u).wait_recv()
        own[u] = own[u] + sib_in[u].astype(jnp.float32)

        @pl.when(not_end)
        def _():
            up_copy(u).wait_recv()
            own[u] = own[u] + up_in[u].astype(jnp.float32)

        in_out[u] = own[u].astype(jnp.bfloat16)

        @pl.when(is_mid)
        def _():
            mid_copy(u).start()

        @pl.when(not_mid)
        def _():
            up_copy(u).start()

    def errors(u):
        @pl.when(is_mid)
        def _():
            mid_copy(u).wait_recv()
            err[rows_of(u, c), :] = (own[u] + mid_in[u].astype(jnp.float32)).astype(jnp.bfloat16)

        @pl.when(not_mid)
        def _():
            out_copy(u).wait_recv()

        @pl.when(not_end)
        def _():
            out_copy(u).start()

        err_copy(u, c).start()

    def collect(u):
        err_copy(u, 1 - c).wait_recv()
        rows = pl.ds(pl.multiple_of(u * unit, unit), unit)
        g_ref[...] += lax.dot_general(
            codes[rows, :], err[rows, :], (((0,), (0,)), ((), ())),
            preferred_element_type=jnp.float32,
        )

    end = lax.max(1 - depth, 0)
    lag_in = (1 - end) * LAG_MID
    lag_err = lag_in + (1 - end) * LAG_ERR + end * LAG_OUTER
    lag_all = lag_err + 1

    @pl.loop(0, units + max(LAG_OUTER, LAG_MID + LAG_ERR) + 1)
    def _(t):
        @pl.when((t < units) & (lax.rem(t, SPLIT) == 0))
        def _():
            compute(t // SPLIT)

        @pl.when((t >= lag_in) & (t < units + lag_in))
        def _():
            relay(t - lag_in)

        @pl.when((t >= lag_err) & (t < units + lag_err))
        def _():
            errors(t - lag_err)

        @pl.when((t >= lag_all) & (t < units + lag_all))
        def _():
            collect(t - lag_all)

    @pl.loop(0, units)
    def _(u):
        sib_copy(u).wait_send()
        up_copy(u).wait_send()
        err_copy(u, c).wait_send()

        @pl.when(not_end)
        def _():
            out_copy(u).wait_send()


def on_device(n, target, dec_w, mom_first, mom_second, ent_row, ent_lat, ent_val, block_count):
    latents, features = dec_w.shape
    slots = ent_row.shape[1]
    rows = target.shape[0] * n * 2
    units = rows // CHUNK * SPLIT
    half = CHUNK // SPLIT // 2
    vmem = pl.BlockSpec(memory_space=pltpu.VMEM)
    block = (units, half, features)
    gradient = pl.pallas_call(
        functools.partial(gradient_kernel, n),
        out_shape=jax.ShapeDtypeStruct((latents, features), jnp.float32),
        in_specs=[pl.BlockSpec(memory_space=pltpu.SMEM)] + [vmem] * 5,
        out_specs=vmem,
        scratch_shapes=[
            pltpu.VMEM((latents, slots), jnp.bfloat16),
            pltpu.VMEM((CHUNK, slots), jnp.bfloat16),
            pltpu.VMEM((rows, latents), jnp.bfloat16),
            pltpu.VMEM((CHUNK, features), jnp.float32),
            pltpu.VMEM(block, jnp.float32),
            pltpu.VMEM((rows, features), jnp.bfloat16),
        ]
        + [pltpu.VMEM(block, jnp.bfloat16)] * 5
        + [pltpu.SemaphoreType.DMA((units,))] * 9,
        compiler_params=pltpu.CompilerParams(
            collective_id=0, has_side_effects=True, vmem_limit_bytes=40 * 2**20
        ),
        cost_estimate=pl.CostEstimate(
            flops=2 * rows * latents * (slots + 2 * features),
            bytes_accessed=6 * latents * features, transcendentals=0,
        ),
    )(block_count, ent_row, ent_lat, ent_val, dec_w, target)
    return adam_apply(dec_w, mom_first, mom_second, gradient)


def solution(mesh):
    shard = P(("groups", "lat", "sub"), "row")
    entries = P(("groups", "lat", "sub"), None)
    return jax.shard_map(
        functools.partial(on_device, mesh.shape["lat"]), mesh=mesh,
        in_specs=(shard, shard, shard, shard, entries, entries, entries, P(("groups", "lat", "sub"))),
        out_specs=(shard, shard, shard), check_vma=False,
    )
```

profile of v0, /device:TPU:1, one launch (start us, length us, event | category | flops | bytes accessed | tf_op | source)
XLA Modules:
  0.0 47.1 jit_solution(720079329181156333)
XLA Ops:
  1.3 0.0 copy-start
  1.3 1.4 %copy-done = bf16[1024,768]{1,0:T(8,128)(2,1)S(1)} copy-done((bf16[1024,768]{1,0:T(8,128)(2,1)S(1)}, bf16[1024,768]{1,0:T(8,128)(2,1)}, u32[]{:S(2)}) %copy-start) | copy-done | bytes 1572888
  2.7 0.0 copy-start.1
  2.7 0.9 %copy-done.1 = bf16[128,768]{1,0:T(8,128)(2,1)S(1)} copy-done((bf16[128,768]{1,0:T(8,128)(2,1)S(1)}, bf16[128,768]{1,0:T(8,128)(2,1)}, u32[]{:S(2)}) %copy-start.1) | copy-done | bytes 196632
  3.6 0.0 copy-start.2
  3.6 0.7 %copy-done.2 = s32[1,2048]{1,0:T(1,128)S(1)} copy-done((s32[1,2048]{1,0:T(1,128)S(1)}, s32[1,2048]{1,0:T(1,128)}, u32[]{:S(2)}) %copy-start.2) | copy-done | bytes 8216
  4.3 0.0 copy-start.3
  4.3 0.7 %copy-done.3 = s32[1,2048]{1,0:T(1,128)S(1)} copy-done((s32[1,2048]{1,0:T(1,128)S(1)}, s32[1,2048]{1,0:T(1,128)}, u32[]{:S(2)}) %copy-start.3) | copy-done | bytes 8216
  5.0 0.0 copy-start.4
  5.0 0.7 %copy-done.4 = bf16[1,2048]{1,0:T(2,128)(2,1)S(1)} copy-done((bf16[1,2048]{1,0:T(2,128)(2,1)S(1)}, bf16[1,2048]{1,0:T(2,128)(2,1)}, u32[]{:S(2)}) %copy-start.4) | copy-done | bytes 4120
  5.7 0.0 copy-start.5
  5.7 0.0 copy-start.6
  5.7 36.5 %shard_map.103 = f32[1024,768]{1,0:T(8,128)S(1)} custom-call(s32[1]{0:T(128)S(6)} %copy.11.count_ref, s32[1,2048]{1,0:T(1,128)S(1)} %copy-done.2, s32[1,2048]{1,0:T(1,128)S(1)} %copy-done.3, bf16[1,2048]{1,0:T(2,128)(2,1)S(1)} %copy-done.4, bf16[1024,768]{1,0:T(8,128)(2,1)S(1)} %copy-done, bf16[128,768]{1,0:T(8,128)(2,1)S(1)} %copy-done.1), custom_call_target="tpu_custom_call" | custom-call | flops 7516192768 | bytes 4718592 | tf_op jit(solution)/shard_map/pallas_call | solution.py:215
  42.2 0.0 copy-done.5
  42.2 0.0 copy-done.6
  42.2 4.9 %fusion.2 = (bf16[1024,768]{1,0:T(8,128)(2,1)}, bf16[1024,768]{1,0:T(8,128)(2,1)}, bf16[1024,768]{1,0:T(8,128)(2,1)}) fusion(f32[1024,768]{1,0:T(8,128)S(1)} %shard_map.103, bf16[1024,768]{1,0:T(8,128)(2,1)S(1)} %copy-done.5, bf16[1024,768]{1,0:T(8,128)(2,1)S(1)} %copy-done.6, bf16[1024,768]{1,0:T(8,128)(2,1)S(1)} %copy-done), kind=kLoop, calls=%fused_computation.5 | loop fusion | flops 14155776 | bytes 12582912 | tf_op jit(solution)/shard_map/convert_element_type | solution.py:33
Async XLA Ops:
  1.3 1.4 %copy-start = (bf16[1024,768]{1,0:T(8,128)(2,1)S(1)}, bf16[1024,768]{1,0:T(8,128)(2,1)}, u32[]{:S(2)}) copy-start(bf16[1024,768]{1,0:T(8,128)(2,1)} %w_ref.1) | copy-start | bytes 4718596
  2.7 0.9 %copy-start.1 = (bf16[128,768]{1,0:T(8,128)(2,1)S(1)}, bf16[128,768]{1,0:T(8,128)(2,1)}, u32[]{:S(2)}) copy-start(bf16[128,768]{1,0:T(8,128)(2,1)} %target_ref.1) | copy-start | bytes 589828
  3.6 0.7 %copy-start.2 = (s32[1,2048]{1,0:T(1,128)S(1)}, s32[1,2048]{1,0:T(1,128)}, u32[]{:S(2)}) copy-start(s32[1,2048]{1,0:T(1,128)} %row_ref.1) | copy-start | bytes 24580
  4.3 0.7 %copy-start.3 = (s32[1,2048]{1,0:T(1,128)S(1)}, s32[1,2048]{1,0:T(1,128)}, u32[]{:S(2)}) copy-start(s32[1,2048]{1,0:T(1,128)} %lat_ref.1) | copy-start | bytes 24580
  5.0 0.7 %copy-start.4 = (bf16[1,2048]{1,0:T(2,128)(2,1)S(1)}, bf16[1,2048]{1,0:T(2,128)(2,1)}, u32[]{:S(2)}) copy-start(bf16[1,2048]{1,0:T(2,128)(2,1)} %val_ref.1) | copy-start | bytes 12292
  5.7 36.5 %copy-start.5 = (bf16[1024,768]{1,0:T(8,128)(2,1)S(1)}, bf16[1024,768]{1,0:T(8,128)(2,1)}, u32[]{:S(2)}) copy-start(bf16[1024,768]{1,0:T(8,128)(2,1)} %param.11) | copy-start | bytes 4718596
  5.7 36.5 %copy-start.6 = (bf16[1024,768]{1,0:T(8,128)(2,1)S(1)}, bf16[1024,768]{1,0:T(8,128)(2,1)}, u32[]{:S(2)}) copy-start(bf16[1024,768]{1,0:T(8,128)(2,1)} %param.10) | copy-start | bytes 4718596
where the time goes:
time: 47.4 us; the launch traced here: 47.1 us
  Pallas kernels  36.5 us (77%)
  other arithmetic  4.88 us (10%)
  local copies, waits for them, and re-layouts  4.42 us (9%)
  between operations  1.32 us (3%)
    pallas_call x1, Pallas kernels, on_device(): pl.pallas_call(functools.partial(gradient_kernel, n), out_shape=jax.Shape...  36.5 us
    convert_element_type x1, other arithmetic, adam_apply(): moment_two.astype(jnp.bfloat16)  4.88 us
    unnamed x14, local copies, waits for them, and re-layouts  4.42 us

commit v1 on v0

--- a/solution.py
+++ b/solution.py
@@ -16,6 +16,7 @@
 correct_one = 0.999973438601112
 correct_two = 0.095207852886291
 
+TILE = 128
 CHUNK = 256
 SPLIT = 2
 LAG_MID = 3
@@ -23,19 +24,45 @@
 LAG_OUTER = 6
 
 
-def adam_apply(weights, first_in, second_in, gradient):
-    moment_one = beta_one * first_in.astype(jnp.float32) + (1.0 - beta_one) * gradient
-    moment_two = beta_two * second_in.astype(jnp.float32) + (1.0 - beta_two) * gradient * gradient
-    update = (
-        learn_rate * (moment_one / correct_one) / (jnp.sqrt(moment_two / correct_two) + epsilon)
-    )
-    new_weights = (weights.astype(jnp.float32) - update).astype(jnp.bfloat16)
-    return (new_weights, moment_one.astype(jnp.bfloat16), moment_two.astype(jnp.bfloat16))
+def adam_kernel(g_ref, w_ref, first_ref, second_ref, w_out, first_out, second_out,
+                w_tile, first_tile, second_tile, sems):
+    tiles = g_ref.shape[0] // TILE
+
+    def copies(k):
+        rows = pl.ds(pl.multiple_of(k * TILE, TILE), TILE)
+        return [
+            pltpu.make_async_copy(tile.at[rows], out.at[rows], sems.at[i, k])
+            for i, (tile, out) in enumerate(
+                ((w_tile, w_out), (first_tile, first_out), (second_tile, second_out)))
+        ]
+
+    @pl.loop(0, tiles)
+    def _(k):
+        rows = pl.ds(pl.multiple_of(k * TILE, TILE), TILE)
+        gradient = g_ref[rows, :]
+        moment_one = (
+            beta_one * first_ref[rows, :].astype(jnp.float32) + (1.0 - beta_one) * gradient
+        )
+        moment_two = beta_two * second_ref[rows, :].astype(jnp.float32) + (
+            ((1.0 - beta_two) * gradient) * gradient
+        )
+        root = lax.rsqrt(moment_two) * moment_two * (1.0 / correct_two) ** 0.5 + epsilon
+        update = (learn_rate / correct_one) * moment_one * pl.reciprocal(root, approx=True)
+        w_tile[rows, :] = (w_ref[rows, :].astype(jnp.float32) - update).astype(jnp.bfloat16)
+        first_tile[rows, :] = moment_one.astype(jnp.bfloat16)
+        second_tile[rows, :] = moment_two.astype(jnp.bfloat16)
+        for copy in copies(k):
+            copy.start()
+
+    @pl.loop(0, tiles)
+    def _(k):
+        for copy in copies(k):
+            copy.wait()
 
 
 def gradient_kernel(
-    n, count_ref, row_ref, lat_ref, val_ref, w_ref, target_ref, g_ref,
-    spread, pick, codes, part, own, err, sib_out, sib_in, in_out, up_in, mid_in,
+    n, count_ref, row_hbm, lat_hbm, val_hbm, w_hbm, target_hbm, g_ref,
+    row_ref, lat_ref, val_ref, w_ref, target_ref, load, spread, pick, codes, part, own, err, sib_out, sib_in, in_out, up_in, mid_in,
     sib_s, sib_r, in_s, up_r, mid_r, out_s, out_r, err_s, err_r,
 ):
     z, c = lax.axis_index("lat"), lax.axis_index("sub")
@@ -51,6 +78,15 @@
     not_end, not_mid = depth > 0, depth < n // 2 - 1
     sib_id, inner_id, outer_id = {"sub": 1 - c}, {"lat": inner}, {"lat": outer}
 
+    loads = [
+        pltpu.make_async_copy(src, dst, load.at[i])
+        for i, (src, dst) in enumerate((
+            (row_hbm, row_ref), (lat_hbm, lat_ref), (val_hbm, val_ref), (w_hbm, w_ref),
+            (target_hbm, target_ref)))
+    ]
+    for copy in loads:
+        copy.start()
+
     barrier = pltpu.get_barrier_semaphore()
     pl.semaphore_signal(barrier, inc=1, device_id=sib_id, device_id_type=MESH)
     pl.semaphore_signal(barrier, inc=1, device_id=inner_id, device_id_type=MESH)
@@ -58,11 +94,15 @@
     @pl.when(not_end)
     def _():
         pl.semaphore_signal(barrier, inc=1, device_id=outer_id, device_id_type=MESH)
-        pl.semaphore_wait(barrier, 3)
-
-    @pl.when(is_end)
-    def _():
-        pl.semaphore_wait(barrier, 2)
+
+    def wait_partners():
+        @pl.when(not_end)
+        def _():
+            pl.semaphore_wait(barrier, 3)
+
+        @pl.when(is_end)
+        def _():
+            pl.semaphore_wait(barrier, 2)
 
     def rows_of(u, which):
         return pl.ds(pl.multiple_of(u * unit + which * half, 16), half)
@@ -91,6 +131,9 @@
         return pltpu.make_async_remote_copy(
             src_ref=err.at[rows_of(u, which)], dst_ref=err.at[rows_of(u, which)],
             send_sem=err_s.at[u], recv_sem=err_r.at[u], device_id=sib_id, device_id_type=MESH)
+
+    for copy in loads[:3]:
+        copy.wait()
 
     live = lax.broadcasted_iota(jnp.int32, (1, slots), 1) < count_ref[0] * BLOCK
     values = jnp.where(live, val_ref[...].astype(jnp.float32), 0.0)
@@ -101,8 +144,6 @@
         spread[pl.ds(pl.multiple_of(k * BLOCK, BLOCK), BLOCK), :] = jnp.where(
             at == lat_ref[...], values, 0.0
         ).astype(jnp.bfloat16)
-
-    g_ref[...] = jnp.zeros_like(g_ref)
 
     def compute(b):
         rows = pl.ds(pl.multiple_of(b * CHUNK, CHUNK), CHUNK)
@@ -111,6 +152,12 @@
         codes[rows, :] = lax.dot_general(
             pick[...], spread[...], (((1,), (1,)), ((), ())), preferred_element_type=jnp.float32
         ).astype(jnp.bfloat16)
+
+        @pl.when(b == 0)
+        def _():
+            for copy in loads[3:]:
+                copy.wait()
+
         part[...] = jnp.dot(codes[rows, :], w_ref[...], preferred_element_type=jnp.float32)
         first = (z * 2 + c) * share
 
@@ -118,6 +165,10 @@
         def _():
             at_own = pl.ds(pl.multiple_of(lax.rem(first, CHUNK), 16), share)
             part[at_own, :] = part[at_own, :] - target_ref[...].astype(jnp.float32)
+
+        @pl.when(b == 0)
+        def _():
+            wait_partners()
 
         for j in range(SPLIT):
             u = b * SPLIT + j
@@ -164,11 +215,14 @@
 
     def collect(u):
         err_copy(u, 1 - c).wait_recv()
-        rows = pl.ds(pl.multiple_of(u * unit, unit), unit)
-        g_ref[...] += lax.dot_general(
-            codes[rows, :], err[rows, :], (((0,), (0,)), ((), ())),
-            preferred_element_type=jnp.float32,
-        )
+
+        @pl.when(lax.rem(u, SPLIT) == SPLIT - 1)
+        def _():
+            rows = pl.ds(pl.multiple_of(u // SPLIT * CHUNK, CHUNK), CHUNK)
+            g_ref[...] += lax.dot_general(
+                codes[rows, :], err[rows, :], (((0,), (0,)), ((), ())),
+                preferred_element_type=jnp.float32,
+            )
 
     end = lax.max(1 - depth, 0)
     lag_in = (1 - end) * LAG_MID
@@ -184,6 +238,10 @@
         @pl.when((t >= lag_in) & (t < units + lag_in))
         def _():
             relay(t - lag_in)
+
+        @pl.when(t == 0)
+        def _():
+            g_ref[...] = jnp.zeros_like(g_ref)
 
         @pl.when((t >= lag_err) & (t < units + lag_err))
         def _():
@@ -210,14 +268,25 @@
     rows = target.shape[0] * n * 2
     units = rows // CHUNK * SPLIT
     half = CHUNK // SPLIT // 2
+    ent_row, ent_lat, ent_val, w_far, target = [
+        pltpu.with_memory_space_constraint(x, pltpu.HBM)
+        for x in (ent_row, ent_lat, ent_val, dec_w, target)
+    ]
+    hbm = pl.BlockSpec(memory_space=pltpu.HBM)
     vmem = pl.BlockSpec(memory_space=pltpu.VMEM)
     block = (units, half, features)
     gradient = pl.pallas_call(
         functools.partial(gradient_kernel, n),
         out_shape=jax.ShapeDtypeStruct((latents, features), jnp.float32),
-        in_specs=[pl.BlockSpec(memory_space=pltpu.SMEM)] + [vmem] * 5,
+        in_specs=[pl.BlockSpec(memory_space=pltpu.SMEM)] + [hbm] * 5,
         out_specs=vmem,
         scratch_shapes=[
+            pltpu.VMEM(ent_row.shape, jnp.int32),
+            pltpu.VMEM(ent_lat.shape, jnp.int32),
+            pltpu.VMEM(ent_val.shape, jnp.bfloat16),
+            pltpu.VMEM(dec_w.shape, jnp.bfloat16),
+            pltpu.VMEM(target.shape, jnp.bfloat16),
+            pltpu.SemaphoreType.DMA((5,)),
             pltpu.VMEM((latents, slots), jnp.bfloat16),
             pltpu.VMEM((CHUNK, slots), jnp.bfloat16),
             pltpu.VMEM((rows, latents), jnp.bfloat16),
@@ -234,8 +303,20 @@
             flops=2 * rows * latents * (slots + 2 * features),
             bytes_accessed=6 * latents * features, transcendentals=0,
         ),
-    )(block_count, ent_row, ent_lat, ent_val, dec_w, target)
-    return adam_apply(dec_w, mom_first, mom_second, gradient)
+    )(block_count, ent_row, ent_lat, ent_val, w_far, target)
+    return pl.pallas_call(
+        adam_kernel,
+        out_shape=[jax.ShapeDtypeStruct((latents, features), jnp.bfloat16)] * 3,
+        in_specs=[vmem] * 4,
+        out_specs=[hbm] * 3,
+        scratch_shapes=[pltpu.VMEM((latents, features), jnp.bfloat16)] * 3
+        + [pltpu.SemaphoreType.DMA((3, latents // TILE))],
+        compiler_params=pltpu.CompilerParams(vmem_limit_bytes=12 * 2**20),
+        cost_estimate=pl.CostEstimate(
+            flops=20 * latents * features, bytes_accessed=16 * latents * features,
+            transcendentals=2 * latents * features,
+        ),
+    )(gradient, dec_w, mom_first, mom_second)
 
 
 def solution(mesh):

time: 47.4 us -> 42.1 us (0.89)
  other arithmetic: 4.88 us -> 0 us
  local copies, waits for them, and re-layouts: 4.42 us -> 0.01 us
  Pallas kernels: 36.5 us -> 40.6 us
    convert_element_type x1 -> x0, other arithmetic: 4.88 us -> none  [adam_apply(): moment_two.astype(jnp.bfloat16)]
    unnamed x14 -> x6, local copies, waits for them, and re-layouts: 4.42 us -> 0.01 us
    pallas_call x0 -> x1, Pallas kernels: none -> 3.17 us  [on_device(): pl.pallas_call(adam_kernel, out_shape=[jax.ShapeDtypeStruct((latents, fea...]
    pallas_call x1, Pallas kernels: 36.5 us -> 37.4 us  [on_device(): pl.pallas_call(functools.partial(gradient_kernel, n), out_shape=jax.Shape...]
where the time goes in v1:
time: 42.1 us; the launch traced here: 41.9 us
  Pallas kernels  40.6 us (96%)
  between operations  1.34 us (3%)
    pallas_call x1, Pallas kernels, on_device(): pl.pallas_call(functools.partial(gradient_kernel, n), out_shape=jax.Shape...  37.4 us
    pallas_call x1, Pallas kernels, on_device(): pl.pallas_call(adam_kernel, out_shape=[jax.ShapeDtypeStruct((latents, fea...  3.17 us

profile of v1, /device:TPU:1, one launch (start us, length us, event | category | flops | bytes accessed | tf_op | source)
XLA Modules:
  0.0 41.9 jit_solution(10850962645232756473)
XLA Ops:
  1.3 0.0 copy-start
  1.3 0.0 copy-start.1
  1.3 0.0 copy-start.2
  1.3 37.4 %shard_map.103.g_ref = f32[1024,768]{1,0:T(8,128)S(1)} custom-call(s32[1]{0:T(128)S(6)} %copy.11.count_ref, s32[1,2048]{1,0:T(1,128)} %row_hbm.1, s32[1,2048]{1,0:T(1,128)} %lat_hbm.1, bf16[1,2048]{1,0:T(2,128)(2,1)} %val_hbm.1, bf16[1024,768]{1,0:T(8,128)(2,1)} %w_ref.1, bf16[128,768]{1,0:T(8,128)(2,1)} %target_hbm.1), custom_call_target="tpu_custom_call" | custom-call | flops 7516192768 | bytes 4718592 | tf_op jit(solution)/shard_map/pallas_call | solution.py:278
  38.7 0.0 copy-done
  38.7 0.0 copy-done.1
  38.7 0.0 copy-done.2
  38.7 3.2 %shard_map.104 = (bf16[1024,768]{1,0:T(8,128)(2,1)}, bf16[1024,768]{1,0:T(8,128)(2,1)}, bf16[1024,768]{1,0:T(8,128)(2,1)}) custom-call(f32[1024,768]{1,0:T(8,128)S(1)} %shard_map.103.g_ref, bf16[1024,768]{1,0:T(8,128)(2,1)S(1)} %copy-done, bf16[1024,768]{1,0:T(8,128)(2,1)S(1)} %copy-done.1, bf16[1024,768]{1,0:T(8,128)(2,1)S(1)} %copy-done.2), custom_call_target="tpu_custom_call" | custom-call | flops 15728640 | bytes 12582912 | tf_op jit(solution)/shard_map/pallas_call | solution.py:307
Async XLA Ops:
  1.3 37.4 %copy-start = (bf16[1024,768]{1,0:T(8,128)(2,1)S(1)}, bf16[1024,768]{1,0:T(8,128)(2,1)}, u32[]{:S(2)}) copy-start(bf16[1024,768]{1,0:T(8,128)(2,1)} %w_ref.1) | copy-start | bytes 4718596
  1.3 37.4 %copy-start.1 = (bf16[1024,768]{1,0:T(8,128)(2,1)S(1)}, bf16[1024,768]{1,0:T(8,128)(2,1)}, u32[]{:S(2)}) copy-start(bf16[1024,768]{1,0:T(8,128)(2,1)} %first_ref.1) | copy-start | bytes 4718596
  1.3 37.4 %copy-start.2 = (bf16[1024,768]{1,0:T(8,128)(2,1)S(1)}, bf16[1024,768]{1,0:T(8,128)(2,1)}, u32[]{:S(2)}) copy-start(bf16[1024,768]{1,0:T(8,128)(2,1)} %second_ref.1) | copy-start | bytes 4718596

commit v2 on v1

--- a/solution.py
+++ b/solution.py
@@ -166,10 +166,6 @@
             at_own = pl.ds(pl.multiple_of(lax.rem(first, CHUNK), 16), share)
             part[at_own, :] = part[at_own, :] - target_ref[...].astype(jnp.float32)
 
-        @pl.when(b == 0)
-        def _():
-            wait_partners()
-
         for j in range(SPLIT):
             u = b * SPLIT + j
             theirs = pl.ds(pl.multiple_of(j * unit + (1 - c) * half, 16), half)
@@ -225,27 +221,29 @@
             )
 
     end = lax.max(1 - depth, 0)
-    lag_in = (1 - end) * LAG_MID
+    lag_in = (1 - end) * LAG_MID + end
     lag_err = lag_in + (1 - end) * LAG_ERR + end * LAG_OUTER
     lag_all = lag_err + 1
 
-    @pl.loop(0, units + max(LAG_OUTER, LAG_MID + LAG_ERR) + 1)
+    wait_partners()
+
+    @pl.loop(0, units + max(LAG_OUTER + 1, LAG_MID + LAG_ERR) + 1)
     def _(t):
+        @pl.when((t >= lag_in) & (t < units + lag_in))
+        def _():
+            relay(t - lag_in)
+
+        @pl.when(t == 0)
+        def _():
+            g_ref[...] = jnp.zeros_like(g_ref)
+
+        @pl.when((t >= lag_err) & (t < units + lag_err))
+        def _():
+            errors(t - lag_err)
+
         @pl.when((t < units) & (lax.rem(t, SPLIT) == 0))
         def _():
             compute(t // SPLIT)
-
-        @pl.when((t >= lag_in) & (t < units + lag_in))
-        def _():
-            relay(t - lag_in)
-
-        @pl.when(t == 0)
-        def _():
-            g_ref[...] = jnp.zeros_like(g_ref)
-
-        @pl.when((t >= lag_err) & (t < units + lag_err))
-        def _():
-            errors(t - lag_err)
 
         @pl.when((t >= lag_all) & (t < units + lag_all))
         def _():

time: 42.1 us -> 42.3 us (level)
  no operation moved by 1% of the time
where the time goes in v2:
time: 42.3 us; the launch traced here: 42.1 us
  Pallas kernels  40.8 us (96%)
  between operations  1.34 us (3%)
    pallas_call x1, Pallas kernels, on_device(): pl.pallas_call(functools.partial(gradient_kernel, n), out_shape=jax.Shape...  37.6 us
    pallas_call x1, Pallas kernels, on_device(): pl.pallas_call(adam_kernel, out_shape=[jax.ShapeDtypeStruct((latents, fea...  3.17 us

profile of v2, /device:TPU:1, one launch (start us, length us, event | category | flops | bytes accessed | tf_op | source)
XLA Modules:
  0.0 42.1 jit_solution(4266933579402323174)
XLA Ops:
  1.3 0.0 copy-start
  1.3 0.0 copy-start.1
  1.3 0.0 copy-start.2
  1.3 37.6 %shard_map.103.g_ref = f32[1024,768]{1,0:T(8,128)S(1)} custom-call(s32[1]{0:T(128)S(6)} %copy.11.count_ref, s32[1,2048]{1,0:T(1,128)} %row_hbm.1, s32[1,2048]{1,0:T(1,128)} %lat_hbm.1, bf16[1,2048]{1,0:T(2,128)(2,1)} %val_hbm.1, bf16[1024,768]{1,0:T(8,128)(2,1)} %w_ref.1, bf16[128,768]{1,0:T(8,128)(2,1)} %target_hbm.1), custom_call_target="tpu_custom_call" | custom-call | flops 7516192768 | bytes 4718592 | tf_op jit(solution)/shard_map/pallas_call | solution.py:276
  38.9 0.0 copy-done
  38.9 0.0 copy-done.1
  38.9 0.0 copy-done.2
  39.0 3.2 %shard_map.104 = (bf16[1024,768]{1,0:T(8,128)(2,1)}, bf16[1024,768]{1,0:T(8,128)(2,1)}, bf16[1024,768]{1,0:T(8,128)(2,1)}) custom-call(f32[1024,768]{1,0:T(8,128)S(1)} %shard_map.103.g_ref, bf16[1024,768]{1,0:T(8,128)(2,1)S(1)} %copy-done, bf16[1024,768]{1,0:T(8,128)(2,1)S(1)} %copy-done.1, bf16[1024,768]{1,0:T(8,128)(2,1)S(1)} %copy-done.2), custom_call_target="tpu_custom_call" | custom-call | flops 15728640 | bytes 12582912 | tf_op jit(solution)/shard_map/pallas_call | solution.py:305
Async XLA Ops:
  1.3 37.6 %copy-start = (bf16[1024,768]{1,0:T(8,128)(2,1)S(1)}, bf16[1024,768]{1,0:T(8,128)(2,1)}, u32[]{:S(2)}) copy-start(bf16[1024,768]{1,0:T(8,128)(2,1)} %w_ref.1) | copy-start | bytes 4718596
  1.3 37.6 %copy-start.1 = (bf16[1024,768]{1,0:T(8,128)(2,1)S(1)}, bf16[1024,768]{1,0:T(8,128)(2,1)}, u32[]{:S(2)}) copy-start(bf16[1024,768]{1,0:T(8,128)(2,1)} %first_ref.1) | copy-start | bytes 4718596
  1.3 37.6 %copy-start.2 = (bf16[1024,768]{1,0:T(8,128)(2,1)S(1)}, bf16[1024,768]{1,0:T(8,128)(2,1)}, u32[]{:S(2)}) copy-start(bf16[1024,768]{1,0:T(8,128)(2,1)} %second_ref.1) | copy-start | bytes 4718596
